TPU v7x, 32 devices: a whole 2x2x4 slice. The times are simulated.
32 devices in a mesh: tm: 8 (over z, core), head: 4 (over y, x).
Axes of the slice: x: 2, y: 2, z: 4, core: 2. Of those that a mesh axis runs over, the one named last changes fastest.
Arguments:
- query: bfloat16 [10240, 12, 128], P(('tm', 'head')), may hold values from -15 to 15
- key: bfloat16 [10240, 12, 128], P(('tm', 'head')), may hold values from -15 to 15
- value: bfloat16 [10240, 12, 128], P(('tm', 'head')), may hold values from -6 to 6
- far_list: int32 [80, 8], P('tm'), may hold values from 0 to 79, as said below
- far_count: int32 [80, 8], P('tm'), may hold values from 0 to 1, as said below
Outputs:
- attended: bfloat16 [10240, 12, 128], P(('tm', 'head'))
Inputs may be any that keep to these rules, and one draw needn't show every extreme that they name: far_list[b, g] is a block of frame g: far_list[b, g] // 10 == g. far_count[b, g] is 0 where the frame of block b and frame g are less than 2 apart. For frames f and g at distance d >= 2, exactly min(5, max(1, 2, 2 * 5 // d)) of the 10 blocks of frame f have far_count 1 for g; so at most 5 blocks of a frame list blocks of one other frame, and exactly 5 at distance 2.
All inputs are finite; a program needn't handle non-finite values.
Results may differ from a plain program's by a relative error of at most 0.012.
Values may be sent and summed in bfloat16 or wider, within the bound.
A program may use at most 128 MiB of HBM per device.

v0:
```python
import functools

import jax
import jax.numpy as jnp
from jax import lax
from jax.experimental import pallas as pl
from jax.experimental.pallas import tpu as pltpu
from jax.sharding import PartitionSpec as P

FW = 80
BLK = 128
RT = 16
RH = 56
RW = 56
CAP = 5
THETA = 256.0
MESH = pl.DeviceIdType.MESH


def quota(gap):
    return min(CAP, max(1, 2 * CAP // 5, 2 * CAP // gap))


def slot_layout(frames):
    sizes = [0] * frames
    for offset in range(1, frames):
        sizes[offset] = max([quota(d) for d in (offset, frames - offset) if d >= 2])
    starts, total = [0] * frames, 0
    for offset in range(1, frames):
        starts[offset] = total
        total += sizes[offset]
    return sizes, starts, total


def swap_matrix(head_width):
    row_ids = jnp.arange(head_width)[:, None]
    col_ids = jnp.arange(head_width)[None, :]
    minus_one = (row_ids == col_ids + 1) & (col_ids % 2 == 0)
    plus_one = (col_ids == row_ids + 1) & (row_ids % 2 == 0)
    return jnp.where(plus_one, 1.0, jnp.where(minus_one, -1.0, 0.0)).astype(jnp.bfloat16)


def axis_angles(positions, span_width):
    pair_index = jnp.arange(span_width // 2).astype(jnp.float32)
    inverse = THETA ** (-2.0 * pair_index / span_width)
    return positions[:, None] * inverse[None, :]


def kernel(
    frames, groups, own_heads, frame_tok, width,
    pick_ref, q_in, k_in, v_in, cos_ref, sin_ref, swap_ref, bias_ref, out_ref,
    *scratch,
):
    sizes, starts, slots = slot_layout(frames)
    span = frame_tok // groups
    blocks = frame_tok // BLK
    own, lo, hi, far = (
        scratch[i * own_heads : (i + 1) * own_heads] for i in range(4)
    )
    (
        q_own, rot_q, rot_k, sent, done,
        in_send, in_recv, in_local, halo_send, halo_recv, far_send, far_recv,
        out_send, out_recv, out_local,
    ) = scratch[4 * own_heads :]
    rings = sent.shape[0]
    frame = lax.axis_index("tm")
    group = lax.axis_index("head")

    for h in range(own_heads):
        far[h][...] = jnp.zeros_like(far[h])

    @pl.when(frame == 0)
    def _():
        for h in range(own_heads):
            lo[h][...] = jnp.zeros_like(lo[h])

    @pl.when(frame == frames - 1)
    def _():
        for h in range(own_heads):
            hi[h][...] = jnp.zeros_like(hi[h])

    barrier = pltpu.get_barrier_semaphore()
    for step in range(1, groups):
        pl.semaphore_signal(
            barrier, inc=1, device_id=(frame, lax.rem(group + step, groups)), device_id_type=MESH
        )
    for step in range(1, frames):
        pl.semaphore_signal(
            barrier, inc=1, device_id=(lax.rem(frame + step, frames), group), device_id_type=MESH
        )
    pl.semaphore_wait(barrier, groups + frames - 2)

    def landing(which, h, source):
        rows = pl.ds(pl.multiple_of(source * span, span), span)
        return q_own.at[h, rows] if which == 2 else own[h].at[which, rows]

    def in_copy(which, h, step):
        peer = lax.rem(group + step, groups)
        source = (rot_k, v_in, rot_q)[which]
        return pltpu.make_async_remote_copy(
            src_ref=source.at[peer * own_heads + h],
            dst_ref=landing(which, h, group),
            send_sem=in_send.at[which, h, step - 1],
            recv_sem=in_recv.at[which, h, step - 1],
            device_id=(frame, peer),
            device_id_type=MESH,
        )

    def in_own(which, h):
        source = (rot_k, v_in, rot_q)[which]
        return pltpu.make_async_copy(
            source.at[group * own_heads + h], landing(which, h, group), in_local.at[which, h]
        )

    def rotate_head(source, target, head):
        x = source[head]
        swapped = jnp.dot(x, swap_ref[...], preferred_element_type=jnp.float32)
        turned = x.astype(jnp.float32) * cos_ref[...] + swapped * sin_ref[...]
        target[head] = turned.astype(jnp.bfloat16)

    for h in range(own_heads):
        for which, (source, target) in ((1, (None, None)), (0, (k_in, rot_k)), (2, (q_in, rot_q))):
            if source is not None:
                for step in range(groups):
                    rotate_head(source, target, step * own_heads + h)
            for step in range(1, groups):
                in_copy(which, h, step).start()
            in_own(which, h).start()

    def in_wait(which, h):
        for step in range(1, groups):
            in_copy(which, h, step).wait_recv()
        in_own(which, h).wait()

    def halo_copy(h, up):
        peer = lax.rem(frame + (1 if up else frames - 1), frames)
        return pltpu.make_async_remote_copy(
            src_ref=own[h],
            dst_ref=(lo if up else hi)[h],
            send_sem=halo_send.at[h, int(up)],
            recv_sem=halo_recv.at[h, int(up)],
            device_id=(peer, group),
            device_id_type=MESH,
        )

    def far_copy(h, offset, count):
        place = pl.ds(starts[offset] * BLK, count * BLK)
        return pltpu.make_async_remote_copy(
            src_ref=sent.at[h % rings, :, place],
            dst_ref=far[h].at[:, place],
            send_sem=far_send.at[h, offset - 1],
            recv_sem=far_recv.at[h, offset - 1],
            device_id=(lax.rem(frame + frames - offset, frames), group),
            device_id_type=MESH,
        )

    def each_far(straight, action, h):
        for offset in range(1, frames):
            direct = straight(offset)
            for condition, gap in ((direct, offset), (jnp.logical_not(direct), frames - offset)):
                if gap >= 2:

                    @pl.when(condition)
                    def _(offset=offset, gap=gap):
                        action(far_copy(h, offset, quota(gap)))

    def sends_far(action, h):
        each_far(lambda offset: frame >= offset, action, h)

    def takes_far(action, h):
        each_far(lambda offset: frame + offset < frames, action, h)

    def sends_halo(action, h):
        @pl.when(frame < frames - 1)
        def _():
            action(halo_copy(h, True))

        @pl.when(frame > 0)
        def _():
            action(halo_copy(h, False))

    def takes_halo(action, h):
        @pl.when(frame > 0)
        def _():
            action(halo_copy(h, True))

        @pl.when(frame < frames - 1)
        def _():
            action(halo_copy(h, False))

    def begin(copy):
        copy.start()

    def wait_send(copy):
        copy.wait_send()

    def wait_recv(copy):
        copy.wait_recv()

    def spread(h):
        in_wait(1, h)
        in_wait(0, h)
        sends_halo(begin, h)
        if h >= rings:
            sends_far(wait_send, h - rings)

        def pick(slot, carry):
            found = jnp.zeros((2, BLK // 16, 16, width), jnp.bfloat16)
            for block in range(blocks):
                part = own[h][:, block * BLK : (block + 1) * BLK, :]
                found = found + part.reshape(found.shape) * pick_ref[slot, block]
            rows = pl.ds(pl.multiple_of(slot * BLK, BLK), BLK)
            sent[h % rings, :, rows, :] = found.reshape(2, BLK, width)
            return carry

        lax.fori_loop(0, slots, pick, 0)
        sends_far(begin, h)

    scale = (width ** -0.5) * 1.4426950408889634
    tile = 2 * BLK
    low_bias = jnp.where(frame > 0, 0.0, -jnp.inf)
    high_bias = jnp.where(frame < frames - 1, 0.0, -jnp.inf)

    def score(rows, keys):
        return lax.dot_general(
            rows, keys, (((1,), (1,)), ((), ())), preferred_element_type=jnp.float32
        )

    def attend(h):
        def one_tile(index, carry):
            rows = q_own[h, pl.ds(pl.multiple_of(index * tile, tile), tile), :]
            near = [
                score(rows, lo[h][0]) + low_bias,
                score(rows, own[h][0]),
                score(rows, hi[h][0]) + high_bias,
            ]
            tops = [jnp.max(part, axis=1, keepdims=True) for part in near]
            top = jnp.maximum(jnp.maximum(tops[0], tops[1]), tops[2])
            found = score(rows, far[h][0]).reshape(2, BLK, slots * BLK)
            found = found + bias_ref[pl.ds(index * 2, 2)]
            found = found.reshape(tile, slots * BLK)
            top = jnp.maximum(top, jnp.max(found, axis=1, keepdims=True))
            total = jnp.zeros((tile, 1), jnp.float32)
            summed = jnp.zeros((tile, width), jnp.float32)
            for part, values in zip(near + [found], (lo[h], own[h], hi[h], far[h])):
                weights = jnp.exp2((part - top) * scale)
                total = total + jnp.sum(weights, axis=1, keepdims=True)
                summed = summed + jnp.dot(
                    weights.astype(jnp.bfloat16), values[1], preferred_element_type=jnp.float32
                )
            done[h, pl.ds(pl.multiple_of(index * tile, tile), tile), :] = (
                summed / total
            ).astype(jnp.bfloat16)
            return carry

        lax.fori_loop(0, frame_tok // tile, one_tile, 0)

    def out_copy(h, step):
        peer = lax.rem(group + step, groups)
        return pltpu.make_async_remote_copy(
            src_ref=done.at[h, pl.ds(pl.multiple_of(peer * span, span), span)],
            dst_ref=out_ref.at[group * own_heads + h],
            send_sem=out_send.at[h, step - 1],
            recv_sem=out_recv.at[h, step - 1],
            device_id=(frame, peer),
            device_id_type=MESH,
        )

    def out_own(h):
        return pltpu.make_async_copy(
            done.at[h, pl.ds(pl.multiple_of(group * span, span), span)],
            out_ref.at[group * own_heads + h],
            out_local.at[h],
        )

    spread(0)
    if own_heads > 1:
        spread(1)
    for h in range(own_heads):
        in_wait(2, h)
        takes_halo(wait_recv, h)
        takes_far(wait_recv, h)
        if h + 2 < own_heads:
            spread(h + 2)
        attend(h)
        for step in range(1, groups):
            out_copy(h, step).start()
        out_own(h).start()

    for h in range(own_heads):
        for which in range(3):
            for step in range(1, groups):
                in_copy(which, h, step).wait_send()
        sends_halo(wait_send, h)
        if h + rings >= own_heads:
            sends_far(wait_send, h)
        for step in range(1, groups):
            out_copy(h, step).wait()
        out_own(h).wait()


def shards(query, key, value, far_list, far_count):
    frames = lax.axis_size("tm")
    groups = lax.axis_size("head")
    frame = lax.axis_index("tm")
    group = lax.axis_index("head")
    span, heads, width = query.shape
    own_heads = heads // groups
    frame_tok = span * groups
    blocks = frame_tok // BLK
    sizes, starts, slots = slot_layout(frames)

    local_ids = jnp.clip(far_list - jnp.arange(frames)[None, :] * blocks, 0, blocks - 1)
    wanted = far_count > 0
    rank = jnp.cumsum(wanted.astype(jnp.int32), axis=0) - 1
    picks = jnp.arange(CAP)[:, None, None]
    asked = jnp.sum(
        jnp.where(wanted[None] & (rank[None] == picks), local_ids[None], 0), axis=1
    ).astype(jnp.int32)
    heard = lax.all_to_all(
        jnp.transpose(asked, (1, 0)), "tm", split_axis=0, concat_axis=0, tiled=True
    )
    offset_of = jnp.array([o for o in range(1, frames) for _ in range(sizes[o])], jnp.int32)
    pick_of = jnp.array([i for o in range(1, frames) for i in range(sizes[o])], jnp.int32)
    requests = heard[(frame - offset_of) % frames, pick_of]
    offsets = jnp.arange(1, frames)
    source = (frame + offsets) % frames
    there = jnp.take(wanted, source, axis=1)
    place = jnp.take(rank, source, axis=1)
    bias = jnp.concatenate(
        [
            jnp.where(
                there[:, o - 1, None] & (place[:, o - 1, None] == jnp.arange(sizes[o])[None, :]),
                0.0,
                -jnp.inf,
            )
            for o in range(1, frames)
        ],
        axis=1,
    ).astype(jnp.float32)
    bias = jnp.repeat(bias, BLK, axis=1)[:, None, :]
    picked = requests[:, None] == jnp.arange(blocks)[None, :]
    picked = jnp.broadcast_to(
        picked.astype(jnp.bfloat16)[:, :, None, None], (slots, blocks, 16, width)
    )

    token = group * span + jnp.arange(span)
    angles = jnp.concatenate(
        [
            axis_angles(jnp.zeros((span,), jnp.float32) + frame.astype(jnp.float32), RT),
            axis_angles((token // FW).astype(jnp.float32), RH),
            axis_angles((token % FW).astype(jnp.float32), RW),
        ],
        axis=1,
    )
    cosines = jnp.repeat(jnp.cos(angles), 2, axis=1)
    sines = jnp.repeat(jnp.sin(angles), 2, axis=1)

    rings = min(own_heads, 3)
    bf16 = jnp.bfloat16
    whole_frame = pltpu.VMEM((2, frame_tok, width), bf16)
    dma = pltpu.SemaphoreType.DMA
    vmem = pl.BlockSpec(memory_space=pltpu.VMEM)
    anywhere = pl.BlockSpec(memory_space=pl.ANY)
    keys_seen = 3 * frame_tok + slots * BLK
    attended = pl.pallas_call(
        functools.partial(kernel, frames, groups, own_heads, frame_tok, width),
        out_shape=jax.ShapeDtypeStruct((heads, span, width), bf16),
        in_specs=[vmem, vmem, vmem, anywhere, vmem, vmem, vmem, vmem],
        out_specs=anywhere,
        scratch_shapes=[whole_frame] * (3 * own_heads)
        + [pltpu.VMEM((2, slots * BLK, width), bf16)] * own_heads
        + [
            pltpu.VMEM((own_heads, frame_tok, width), bf16),
            pltpu.VMEM((heads, span, width), bf16),
            pltpu.VMEM((heads, span, width), bf16),
            pltpu.VMEM((rings, 2, slots * BLK, width), bf16),
            pltpu.VMEM((own_heads, frame_tok, width), bf16),
            dma((3, own_heads, groups - 1)),
            dma((3, own_heads, groups - 1)),
            dma((3, own_heads)),
            dma((own_heads, 2)),
            dma((own_heads, 2)),
            dma((own_heads, frames - 1)),
            dma((own_heads, frames - 1)),
            dma((own_heads, groups - 1)),
            dma((own_heads, groups - 1)),
            dma((own_heads,)),
        ],
        compiler_params=pltpu.CompilerParams(
            collective_id=0, has_side_effects=True, vmem_limit_bytes=62 * 1024 * 1024
        ),
        cost_estimate=pl.CostEstimate(
            flops=4 * own_heads * frame_tok * keys_seen * width,
            bytes_accessed=8 * heads * span * width,
            transcendentals=own_heads * frame_tok * keys_seen,
        ),
    )(
        picked,
        jnp.transpose(query, (1, 0, 2)),
        jnp.transpose(key, (1, 0, 2)),
        jnp.transpose(value, (1, 0, 2)),
        cosines,
        sines,
        swap_matrix(width),
        bias,
    )
    return jnp.transpose(attended, (1, 0, 2))


def solution(mesh):
    in_specs = (
        P(("tm", "head"), None, None),
        P(("tm", "head"), None, None),
        P(("tm", "head"), None, None),
        P("tm", None),
        P("tm", None),
    )
    out_specs = P(("tm", "head"), None, None)
    return jax.shard_map(shards, mesh=mesh, in_specs=in_specs, out_specs=out_specs, check_vma=False)
```

profile of v0, /device:TPU:0, one launch (start us, length us, event | category | flops | bytes accessed | tf_op | source)
XLA Modules:
  0.0 167.2 jit_solution(8735306172209194364)
XLA Ops:
  0.0 0.7 fusion.35
  0.7 0.0 copy-start
  0.7 0.2 reduce_window_sum.11
  0.9 0.5 copy-done
  1.4 0.1 subtract_clamp_fusion
  1.5 0.2 select_reduce_fusion
  1.6 0.7 copy.23
  2.3 6.3 %all-to-all-start = ((s32[8,1,5]{2,1,0:T(1,128)}), s32[8,1,5]{2,1,0:T(1,128)S(1)}, u32[]{:S(2)}, u32[]{:S(2)}) async-start(s32[8,1,5]{2,1,0:T(1,128)} %copy.23), calls=%async_computation | async-start | bytes 8192 | tf_op jit(solution)/shard_map/all_to_all | solution.py:320
  8.7 0.6 gather_fusion.1
  9.3 0.6 gather_fusion.2
  9.9 0.1 select_bitcast_fusion.1
  10.0 0.1 select_bitcast_fusion
  10.1 0.1 broadcast_multiply_fusion.1
  10.1 0.4 fusion
  10.5 0.1 broadcast_in_dim.123
  10.6 0.1 reshape.174
  10.8 0.0 copy-start.1
  10.8 0.0 copy-start.2
  10.8 0.8 copy.25.sin_ref
  11.6 0.0 copy-done.1
  11.6 0.0 copy-done.2
  11.6 0.1 fusion.19
  11.7 0.1 fusion.17
  11.7 0.1 fusion.15
  11.8 0.1 fusion.13
  11.9 0.1 fusion.11
  12.0 0.1 fusion.9
  12.0 0.1 fusion.7
  12.1 0.7 select_convert_fusion.swap_ref
  12.8 0.1 concatenate.11
  12.9 0.1 broadcast_in_dim.136
  13.0 0.8 broadcast_in_dim_reshape.3.bias_ref
  13.8 0.1 broadcast_in_dim.122
  13.8 0.1 reshape.173
  14.0 0.8 copy.24.cos_ref
  14.8 0.0 all-to-all-done
  14.8 0.7 gather_fusion
  15.5 0.1 fusion.5
  15.6 1.2 broadcast_in_dim.121.pick_ref
  16.8 148.1 %shard_map.73 = bf16[12,320,128]{2,1,0:T(8,128)(2,1)} custom-call(bf16[22,10,16,128]{3,2,1,0:T(8,128)(2,1)} %broadcast_in_dim.121.pick_ref, bf16[12,320,128]{2,1,0:T(8,128)(2,1)} %bitcast.49, bf16[12,320,128]{2,1,0:T(8,128)(2,1)} %bitcast.50, bf16[12,320,128]{2,1,0:T(8,128)(2,1)} %bitcast.51, f32[320,128]{1,0:T(8,128)} %copy.24.cos_ref, ...), custom_call_target="tpu_custom_call" | custom-call | flops 13086228480 | bytes 3932160 | tf_op jit(solution)/shard_map/pallas_call | solution.py:366
  165.0 2.2 %copy.29 = bf16[320,12,128]{2,0,1:T(8,128)(2,1)} copy(bf16[320,12,128]{2,0,1:T(8,128)(2,1)} %bitcast.47) | data formatting | bytes 1966080
  (13 shorter events, 0.1 us)
Async XLA Ops:
  0.7 0.7 copy-start
  2.3 12.5 %all-to-all-start = ((s32[8,1,5]{2,1,0:T(1,128)}), s32[8,1,5]{2,1,0:T(1,128)S(1)}, u32[]{:S(2)}, u32[]{:S(2)}) async-start(s32[8,1,5]{2,1,0:T(1,128)} %copy.23), calls=%async_computation | async-start | bytes 8192 | tf_op jit(solution)/shard_map/all_to_all | solution.py:320
  10.8 0.8 copy-start.1
  10.8 0.8 copy-start.2
where the time goes:
time: 167 us
  Pallas kernels  148 us (89%)
  local copies, waits for them, and re-layouts  9.45 us (6%)
  starting transfers between devices  6.33 us (4%)
  other arithmetic  3.12 us (2%)
    pallas_call x1, Pallas kernels, shards(): pl.pallas_call(functools.partial(kernel, frames, groups, own_heads, frame...  148 us
    all_to_all x1, starting transfers between devices, shards(): lax.all_to_all(jnp.transpose(asked, (1, 0)), 'tm', split_axis=0, concat_a...  6.33 us
  transfers between devices with their start and end apart: 1, of which 0 were waited for; matrix products, arithmetic and copies ran while one was open for 4% of the time, Pallas kernels for 0%

commit v1 on v0

--- a/solution.py
+++ b/solution.py
@@ -273,15 +273,14 @@
             out_local.at[h],
         )
 
-    spread(0)
-    if own_heads > 1:
-        spread(1)
+    for h in range(min(own_heads, 3)):
+        spread(h)
     for h in range(own_heads):
         in_wait(2, h)
         takes_halo(wait_recv, h)
         takes_far(wait_recv, h)
-        if h + 2 < own_heads:
-            spread(h + 2)
+        if h + 3 < own_heads:
+            spread(h + 3)
         attend(h)
         for step in range(1, groups):
             out_copy(h, step).start()

time: 167 us -> 167 us (level)
  no operation moved by 1% of the time
where the time goes in v1:
time: 167 us
  Pallas kernels  148 us (89%)
  local copies, waits for them, and re-layouts  9.45 us (6%)
  starting transfers between devices  6.33 us (4%)
  other arithmetic  3.12 us (2%)
    pallas_call x1, Pallas kernels, shards(): pl.pallas_call(functools.partial(kernel, frames, groups, own_heads, frame...  148 us
    all_to_all x1, starting transfers between devices, shards(): lax.all_to_all(jnp.transpose(asked, (1, 0)), 'tm', split_axis=0, concat_a...  6.33 us
  transfers between devices with their start and end apart: 1, of which 0 were waited for; matrix products, arithmetic and copies ran while one was open for 4% of the time, Pallas kernels for 0%

profile of v1, /device:TPU:0, one launch (start us, length us, event | category | flops | bytes accessed | tf_op | source)
XLA Modules:
  0.0 167.2 jit_solution(15452578728291060260)
XLA Ops:
  0.0 0.7 fusion.35
  0.7 0.0 copy-start
  0.7 0.2 reduce_window_sum.11
  0.9 0.5 copy-done
  1.4 0.1 subtract_clamp_fusion
  1.5 0.2 select_reduce_fusion
  1.6 0.7 copy.23
  2.3 6.3 %all-to-all-start = ((s32[8,1,5]{2,1,0:T(1,128)}), s32[8,1,5]{2,1,0:T(1,128)S(1)}, u32[]{:S(2)}, u32[]{:S(2)}) async-start(s32[8,1,5]{2,1,0:T(1,128)} %copy.23), calls=%async_computation | async-start | bytes 8192 | tf_op jit(solution)/shard_map/all_to_all | solution.py:319
  8.7 0.6 gather_fusion.1
  9.3 0.6 gather_fusion.2
  9.9 0.1 select_bitcast_fusion.1
  10.0 0.1 select_bitcast_fusion
  10.1 0.1 broadcast_multiply_fusion.1
  10.1 0.4 fusion
  10.5 0.1 broadcast_in_dim.123
  10.6 0.1 reshape.174
  10.8 0.0 copy-start.1
  10.8 0.0 copy-start.2
  10.8 0.8 copy.25.sin_ref
  11.6 0.0 copy-done.1
  11.6 0.0 copy-done.2
  11.6 0.1 fusion.19
  11.7 0.1 fusion.17
  11.7 0.1 fusion.15
  11.8 0.1 fusion.13
  11.9 0.1 fusion.11
  12.0 0.1 fusion.9
  12.0 0.1 fusion.7
  12.1 0.7 select_convert_fusion.swap_ref
  12.8 0.1 concatenate.11
  12.9 0.1 broadcast_in_dim.136
  13.0 0.8 broadcast_in_dim_reshape.3.bias_ref
  13.8 0.1 broadcast_in_dim.122
  13.8 0.1 reshape.173
  14.0 0.8 copy.24.cos_ref
  14.8 0.0 all-to-all-done
  14.8 0.7 gather_fusion
  15.5 0.1 fusion.5
  15.6 1.2 broadcast_in_dim.121.pick_ref
  16.8 148.1 %shard_map.73 = bf16[12,320,128]{2,1,0:T(8,128)(2,1)} custom-call(bf16[22,10,16,128]{3,2,1,0:T(8,128)(2,1)} %broadcast_in_dim.121.pick_ref, bf16[12,320,128]{2,1,0:T(8,128)(2,1)} %bitcast.49, bf16[12,320,128]{2,1,0:T(8,128)(2,1)} %bitcast.50, bf16[12,320,128]{2,1,0:T(8,128)(2,1)} %bitcast.51, f32[320,128]{1,0:T(8,128)} %copy.24.cos_ref, ...), custom_call_target="tpu_custom_call" | custom-call | flops 13086228480 | bytes 3932160 | tf_op jit(solution)/shard_map/pallas_call | solution.py:365
  165.0 2.2 %copy.29 = bf16[320,12,128]{2,0,1:T(8,128)(2,1)} copy(bf16[320,12,128]{2,0,1:T(8,128)(2,1)} %bitcast.47) | data formatting | bytes 1966080
  (13 shorter events, 0.1 us)
Async XLA Ops:
  0.7 0.7 copy-start
  2.3 12.5 %all-to-all-start = ((s32[8,1,5]{2,1,0:T(1,128)}), s32[8,1,5]{2,1,0:T(1,128)S(1)}, u32[]{:S(2)}, u32[]{:S(2)}) async-start(s32[8,1,5]{2,1,0:T(1,128)} %copy.23), calls=%async_computation | async-start | bytes 8192 | tf_op jit(solution)/shard_map/all_to_all | solution.py:319
  10.8 0.8 copy-start.1
  10.8 0.8 copy-start.2
